TPU v7x, 32 devices: a whole 2x2x4 slice. The times are simulated.
32 devices in a mesh: groups: 2 (over y), ctx: 8 (over z, x), sub: 2 (over core).
Axes of the slice: x: 2, y: 2, z: 4, core: 2. Of those that a mesh axis runs over, the one named last changes fastest.
Arguments:
- queries: bfloat16 [2048, 1024], P(('groups', 'ctx'), 'sub'), parts along dimension 0, may hold values from -6 to 6
- key_vectors: bfloat16 [2048, 128], P(('groups', 'ctx')), parts along dimension 0, may hold values from -6 to 6
- value_vectors: bfloat16 [2048, 128], P(('groups', 'ctx')), parts along dimension 0, may hold values from -6 to 6
- attn_output: bfloat16 [2048, 1024], P(('groups', 'ctx'), 'sub'), parts along dimension 0, may hold values from -6 to 6
- grad_output: bfloat16 [2048, 1024], P(('groups', 'ctx'), 'sub'), parts along dimension 0, may hold values from -4 to 4
- row_logsum: float32 [8, 2048], P('sub', ('groups', 'ctx')), parts along dimension 1, may hold values from -0.5 to 7
- block_place: int32 [16], P('groups'), parts along dimension 0, may hold values from 0 to 7, as said below
Outputs:
- grad_queries: bfloat16 [2048, 1024], P(('groups', 'ctx'), 'sub'), parts along dimension 0
- grad_keys: bfloat16 [2048, 128], P(('groups', 'ctx')), parts along dimension 0
- grad_values: bfloat16 [2048, 128], P(('groups', 'ctx')), parts along dimension 0
There are 2 independent parts, one for each index of `groups`. A program takes and returns all parts, laid end to end along the dimension named above; each array names one. Nothing has to cross between parts.
Inputs may be any that keep to these rules, and one draw needn't show every extreme that they name: `block_place`: a permutation of 0 to 7.
All inputs are finite; a program needn't handle non-finite values.
Results may differ from a plain program's by a relative error of at most 0.0055.
Values may be sent and summed in bfloat16 or wider, within the bound.
A program may use at most 64 MiB of HBM per device.

v0:
```python
import jax
import jax.numpy as jnp
from jax import lax
from jax.sharding import PartitionSpec as P


def partner(value, axis, distance):
    mask = 2**distance
    pairs = [(source, source ^ mask) for source in range(lax.axis_size(axis))]
    return lax.ppermute(value, axis, pairs)


def table_lookup(table, wanted):
    slot_ids = jnp.arange(table.shape[0], dtype=jnp.int32)
    return jnp.sum(jnp.where(wanted[:, None] == slot_ids[None, :], table[None, :], 0), axis=1)


def double_up(pieces, extra):
    return tuple((jnp.concatenate([mine, theirs], axis=0) for mine, theirs in zip(pieces, extra)))


def reduce_keys(key_sum, value_sum, first_bit):
    for section_bit in reversed(range(key_sum.shape[0].bit_length() - 1)):
        halfway = 1 << section_bit
        far_key, far_value = partner(
            (key_sum[halfway:], value_sum[halfway:]), "ctx", first_bit + section_bit
        )
        key_sum = key_sum[:halfway] + far_key
        value_sum = value_sum[:halfway] + far_value
    return (key_sum[0], value_sum[0])


def per_device(
    queries, key_vectors, value_vectors, attn_output, grad_output, row_logsum, block_place
):
    ctx_count = lax.axis_size("ctx")
    bit_count = ctx_count.bit_length() - 1
    row_bits = (bit_count + 1) // 2
    own_index = lax.axis_index("ctx")
    tokens = queries.shape[0]
    head_size = key_vectors.shape[1]
    head_count = row_logsum.shape[0]
    score_scale = head_size ** (-0.5)
    row_delta = jnp.einsum(
        "thd,thd->ht",
        grad_output.reshape(tokens, head_count, head_size),
        attn_output.reshape(tokens, head_count, head_size),
        preferred_element_type=jnp.float32,
    )
    row_query, row_grad = (queries[None], grad_output[None])
    row_lse_all, row_delta_all = (row_logsum[None], row_delta[None])
    for section_bit in range(row_bits):
        far_query, far_grad = partner((row_query, row_grad), "ctx", section_bit)
        far_lse, far_delta = partner((row_lse_all, row_delta_all), "ctx", section_bit)
        row_query, row_grad = double_up((row_query, row_grad), (far_query, far_grad))
        row_lse_all, row_delta_all = double_up((row_lse_all, row_delta_all), (far_lse, far_delta))
    col_key, col_value = (key_vectors[None], value_vectors[None])
    for section_bit in range(row_bits, bit_count):
        far_key, far_value = partner((col_key, col_value), "ctx", section_bit)
        col_key, col_value = double_up((col_key, col_value), (far_key, far_value))
    row_total = 1 << row_bits
    col_total = 1 << bit_count - row_bits
    pair_width = min(2, col_total)
    group_count = col_total // pair_width
    group_rows = pair_width * tokens
    row_blocks = table_lookup(
        block_place, jnp.bitwise_xor(own_index, jnp.arange(row_total, dtype=jnp.int32))
    )
    col_blocks = table_lookup(
        block_place, jnp.bitwise_xor(own_index, jnp.arange(col_total, dtype=jnp.int32) * row_total)
    )
    offsets = jnp.arange(tokens, dtype=jnp.int32)
    group_place = (col_blocks[:, None] * tokens + offsets[None, :]).reshape(group_count, group_rows)
    group_first = jnp.min(col_blocks.reshape(group_count, pair_width), axis=1)
    key_groups = col_key.reshape(group_count, group_rows, head_size)
    value_groups = col_value.reshape(group_count, group_rows, head_size)
    row_tiles = row_query.reshape(row_total, tokens, head_count, head_size)
    grad_tiles = row_grad.reshape(row_total, tokens, head_count, head_size)

    def row_sweep(key_state, row_index):
        query_tile = row_tiles[row_index]
        grad_tile = grad_tiles[row_index]
        lse_tile = row_lse_all[row_index].T
        delta_tile = row_delta_all[row_index].T
        row_block = row_blocks[row_index]
        row_place = row_block * tokens + offsets

        def group_sweep(tile_state, group_index):

            def visible(state):
                query_acc, key_acc, value_acc = state
                key_tile = key_groups[group_index]
                value_tile = value_groups[group_index]
                col_place = group_place[group_index]
                scores = (
                    jnp.einsum(
                        "thd,kd->thk", query_tile, key_tile, preferred_element_type=jnp.float32
                    )
                    * score_scale
                )
                allowed = col_place[None, None, :] <= row_place[:, None, None]
                attn_prob = jnp.where(allowed, jnp.exp(scores - lse_tile[:, :, None]), 0.0)
                prob_half = attn_prob.astype(jnp.bfloat16)
                grad_prob = jnp.einsum(
                    "thd,kd->thk", grad_tile, value_tile, preferred_element_type=jnp.float32
                )
                grad_score = (attn_prob * (grad_prob - delta_tile[:, :, None])).astype(jnp.bfloat16)
                query_acc = query_acc + jnp.einsum(
                    "thk,kd->thd", grad_score, key_tile, preferred_element_type=jnp.float32
                )
                key_term = jnp.einsum(
                    "thk,thd->kd", grad_score, query_tile, preferred_element_type=jnp.float32
                )
                value_term = jnp.einsum(
                    "thk,thd->kd", prob_half, grad_tile, preferred_element_type=jnp.float32
                )
                key_acc = key_acc.at[group_index].add(key_term)
                value_acc = value_acc.at[group_index].add(value_term)
                return (query_acc, key_acc, value_acc)

            tile_state = lax.cond(
                group_first[group_index] <= row_block, visible, lambda state: state, tile_state
            )
            return (tile_state, None)

        query_zero = jnp.zeros((tokens, head_count, head_size), jnp.float32)
        start_state = (query_zero, key_state[0], key_state[1])
        (query_acc, key_acc, value_acc), unused = lax.scan(
            group_sweep, start_state, jnp.arange(group_count, dtype=jnp.int32)
        )
        return ((key_acc, value_acc), query_acc)

    kv_zero = jnp.zeros((group_count, group_rows, head_size), jnp.float32)
    (key_grouped, value_grouped), query_terms = lax.scan(
        row_sweep, (kv_zero, kv_zero), jnp.arange(row_total, dtype=jnp.int32)
    )
    key_total = key_grouped.reshape(col_total, tokens, head_size)
    value_total = value_grouped.reshape(col_total, tokens, head_size)
    query_sum = query_terms
    for section_bit in reversed(range(row_bits)):
        halfway = 1 << section_bit
        query_sum = query_sum[:halfway] + partner(query_sum[halfway:], "ctx", section_bit)
    grad_queries = (
        (query_sum[0] * score_scale).reshape(tokens, head_count * head_size).astype(jnp.bfloat16)
    )
    key_sum, value_sum = reduce_keys(key_total, value_total, row_bits)
    key_sum, value_sum = lax.psum((key_sum, value_sum), "sub")
    grad_keys = (key_sum * score_scale).astype(jnp.bfloat16)
    grad_values = value_sum.astype(jnp.bfloat16)
    return (grad_queries, grad_keys, grad_values)


def solution(mesh):
    placed = (
        P(("groups", "ctx"), "sub"),
        P(("groups", "ctx"), None),
        P(("groups", "ctx"), None),
        P(("groups", "ctx"), "sub"),
        P(("groups", "ctx"), "sub"),
        P("sub", ("groups", "ctx")),
        P("groups"),
    )
    return jax.shard_map(
        per_device,
        mesh=mesh,
        in_specs=placed,
        out_specs=(
            P(("groups", "ctx"), "sub"),
            P(("groups", "ctx"), None),
            P(("groups", "ctx"), None),
        ),
        check_vma=False,
    )
```

profile of v0, /device:TPU:1, one launch (start us, length us, event | category | flops | bytes accessed | tf_op | source)
XLA Modules:
  0.0 103.3 jit_solution(7321975807433112288)
XLA Ops:
  7.2 2.1 %collective-permute-start = (f32[1,4,128]{2,1,0:T(4,128)}, f32[1,4,128]{2,1,0:T(4,128)S(1)}, u32[]{:S(2)}, u32[]{:S(2)}) collective-permute-start(f32[1,4,128]{2,1,0:T(4,128)} %bitcast.110), channel_id=1, source_target_pairs={{0,2},{2,0},{4,6},{6,4},{8,10},{10,8},{12,14},{14,12},{1,3},{3,1},... | collective-permute-start | bytes 6152 | tf_op jit(solution)/shard_map/ppermute | solution.py:10
  9.3 2.3 %collective-permute-start.6 = (bf16[1,128,128]{2,1,0:T(8,128)(2,1)}, bf16[1,128,128]{2,1,0:T(8,128)(2,1)S(1)}, u32[]{:S(2)}, u32[]{:S(2)}) collective-permute-start(bf16[1,128,128]{2,1,0:T(8,128)(2,1)} %bitcast.101), channel_id=1, source_target_pairs={{0,8},{2,10},{4,12},{6,14},{8,0},{10,2},{12,4},{14,6},{1,9},{3,11}... | collective-permute-start | bytes 98312 | tf_op jit(solution)/shard_map/ppermute | solution.py:10
  11.7 1.0 reshape.178
  13.4 1.3 %collective-permute-start.7 = (bf16[1,128,512]{1,2,0:T(8,128)(2,1)S(1)}, bf16[1,128,512]{1,2,0:T(8,128)(2,1)S(1)}, u32[]{:S(2)}, u32[]{:S(2)}) collective-permute-start(bf16[1,128,512]{1,2,0:T(8,128)(2,1)S(1)} %bitcast.89), channel_id=1, source_target_pairs={{0,2},{2,0},{4,6},{6,4},{8,10},{10,8},{12,14},{14,12},{1,3},{3,1},... | collective-permute-start | bytes 393224 | tf_op jit(solution)/shard_map/ppermute | solution.py:10
  17.0 1.3 %collective-permute-start.1 = (f32[2,4,128]{2,1,0:T(4,128)S(1)}, f32[2,4,128]{2,1,0:T(4,128)S(1)}, u32[]{:S(2)}, u32[]{:S(2)}) collective-permute-start(f32[2,4,128]{2,1,0:T(4,128)S(1)} %pad_maximum_fusion.8), channel_id=1, source_target_pairs={{0,4},{2,6},{4,0},{6,2},{8,12},{10,14},{12,8},{14,10},{1,5},{3,7},... | collective-permute-start | bytes 12296 | tf_op jit(solution)/shard_map/ppermute | solution.py:10
  18.4 1.4 %collective-permute-done.1 = f32[2,4,128]{2,1,0:T(4,128)S(1)} collective-permute-done((f32[2,4,128]{2,1,0:T(4,128)S(1)}, f32[2,4,128]{2,1,0:T(4,128)S(1)}, u32[]{:S(2)}, u32[]{:S(2)}) %collective-permute-start.1) | collective-permute-done | bytes 4128 | tf_op jit(solution)/shard_map/ppermute | solution.py:10
  19.8 1.3 %collective-permute-start.3 = (f32[2,4,128]{2,1,0:T(4,128)S(1)}, f32[2,4,128]{2,1,0:T(4,128)S(1)}, u32[]{:S(2)}, u32[]{:S(2)}) collective-permute-start(f32[2,4,128]{2,1,0:T(4,128)S(1)} %pad_maximum_fusion.9), channel_id=1, source_target_pairs={{0,4},{2,6},{4,0},{6,2},{8,12},{10,14},{12,8},{14,10},{1,5},{3,7},... | collective-permute-start | bytes 12296 | tf_op jit(solution)/shard_map/ppermute | solution.py:10
  21.1 1.4 %collective-permute-done.3 = f32[2,4,128]{2,1,0:T(4,128)S(1)} collective-permute-done((f32[2,4,128]{2,1,0:T(4,128)S(1)}, f32[2,4,128]{2,1,0:T(4,128)S(1)}, u32[]{:S(2)}, u32[]{:S(2)}) %collective-permute-start.3) | collective-permute-done | bytes 4128 | tf_op jit(solution)/shard_map/ppermute | solution.py:10
  22.6 1.4 %collective-permute-start.8 = (bf16[2,128,512]{1,2,0:T(8,128)(2,1)S(1)}, bf16[2,128,512]{1,2,0:T(8,128)(2,1)S(1)}, u32[]{:S(2)}, u32[]{:S(2)}) collective-permute-start(bf16[2,128,512]{1,2,0:T(8,128)(2,1)S(1)} %pad_maximum_fusion.3), channel_id=1, source_target_pairs={{0,4},{2,6},{4,0},{6,2},{8,12},{10,14},{12,8},{14,10},{1,5},{3,7},... | collective-permute-start | bytes 786440 | tf_op jit(solution)/shard_map/ppermute | solution.py:10
  24.8 3.1 %collective-permute-done.8 = bf16[2,128,512]{1,2,0:T(8,128)(2,1)S(1)} collective-permute-done((bf16[2,128,512]{1,2,0:T(8,128)(2,1)S(1)}, bf16[2,128,512]{1,2,0:T(8,128)(2,1)S(1)}, u32[]{:S(2)}, u32[]{:S(2)}) %collective-permute-start.8) | collective-permute-done | bytes 262176 | tf_op jit(solution)/shard_map/ppermute | solution.py:10
  28.3 4.1 %collective-permute-done.5 = bf16[2,128,512]{1,2,0:T(8,128)(2,1)S(1)} collective-permute-done((bf16[2,128,512]{1,2,0:T(8,128)(2,1)S(1)}, bf16[2,128,512]{1,2,0:T(8,128)(2,1)S(1)}, u32[]{:S(2)}, u32[]{:S(2)}) %collective-permute-start.5) | collective-permute-done | bytes 262176 | tf_op jit(solution)/shard_map/ppermute | solution.py:10
  32.7 22.8 %while.17 = (s32[]{:T(128)}, f32[1,256,128]{2,1,0:T(8,128)S(1)}, f32[1,256,128]{2,1,0:T(8,128)S(1)}, f32[4,128,4,128]{3,1,2,0:T(8,128)S(1)}, s32[1]{0:T(128)}, /...) while((s32[]{:T(128)}, f32[1,256,128]{2,1,0:T(8,128)S(1)}, ...), condition=%wide.region_7.8_spmd.clone, body=%wide.region_3.7_spmd.clone.sunk | while | flops 168853888 | bytes 5259717 | solution.py:134
  35.3 0.7 dynamic_slice.62
  37.4 2.1 %conditional.3 = (f32[1,256,128]{2,1,0:T(8,128)S(1)}, f32[1,256,128]{2,1,0:T(8,128)S(1)}, f32[1,128,4,128]{3,1,2,0:T(8,128)S(1)}) conditional(s32[]{:T(128)} %convert_element_type.35, (f32[1,256,128]{2,1,0:T(8,128)S(1)}, f32[1,256,128]{2,1,0:T(8,128)S(1)}, f32[128,4,128]{2,0,1:T(8,128)S(1)}) %tuple.69, (s32[1,256]{1,0:T(1,128)S(1)}, s32[]{:T(128)}, ...), branch_computations={%region_4.4_spmd, %region_5.6_spmd} | conditional | flops 168853632 | bytes 4201016 | solution.py:121
  53.4 2.1 %conditional.3 = (f32[1,256,128]{2,1,0:T(8,128)S(1)}, f32[1,256,128]{2,1,0:T(8,128)S(1)}, f32[1,128,4,128]{3,1,2,0:T(8,128)S(1)}) conditional(s32[]{:T(128)} %convert_element_type.35, (f32[1,256,128]{2,1,0:T(8,128)S(1)}, f32[1,256,128]{2,1,0:T(8,128)S(1)}, f32[128,4,128]{2,0,1:T(8,128)S(1)}) %tuple.69, (s32[1,256]{1,0:T(1,128)S(1)}, s32[]{:T(128)}, ...), branch_computations={%region_4.4_spmd, %region_5.6_spmd} | conditional | flops 168853632 | bytes 4201016 | solution.py:121
  55.6 5.4 %collective-permute-start.10 = (f32[2,128,4,128]{3,1,2,0:T(8,128)S(1)}, f32[2,128,4,128]{3,1,2,0:T(8,128)S(1)}, u32[]{:S(2)}, u32[]{:S(2)}) collective-permute-start(f32[2,128,4,128]{3,1,2,0:T(8,128)S(1)} %slice.67), channel_id=1, source_target_pairs={{0,4},{2,6},{4,0},{6,2},{8,12},{10,14},{12,8},{14,10},{1,5},{3,7},... | collective-permute-start | bytes 1572872 | tf_op jit(solution)/shard_map/ppermute | solution.py:10
  60.9 2.2 %collective-permute-start.12 = (f32[1,128,128]{2,1,0:T(8,128)S(1)}, f32[1,128,128]{2,1,0:T(8,128)S(1)}, u32[]{:S(2)}, u32[]{:S(2)}) collective-permute-start(f32[1,128,128]{2,1,0:T(8,128)S(1)} %slice.71), channel_id=1, source_target_pairs={{0,8},{2,10},{4,12},{6,14},{8,0},{10,2},{12,4},{14,6},{1,9},{3,11}... | collective-permute-start | bytes 196616 | tf_op jit(solution)/shard_map/ppermute | solution.py:10
  63.3 5.5 %collective-permute-done.12 = f32[1,128,128]{2,1,0:T(8,128)S(1)} collective-permute-done((f32[1,128,128]{2,1,0:T(8,128)S(1)}, f32[1,128,128]{2,1,0:T(8,128)S(1)}, u32[]{:S(2)}, u32[]{:S(2)}) %collective-permute-start.12) | collective-permute-done | bytes 65568 | tf_op jit(solution)/shard_map/ppermute | solution.py:10
  69.5 0.7 collective-permute-done.13
  70.2 1.3 %collective-permute-done.10 = f32[2,128,4,128]{3,1,2,0:T(8,128)S(1)} collective-permute-done((f32[2,128,4,128]{3,1,2,0:T(8,128)S(1)}, f32[2,128,4,128]{3,1,2,0:T(8,128)S(1)}, u32[]{:S(2)}, u32[]{:S(2)}) %collective-permute-start.10) | collective-permute-done | bytes 524320 | tf_op jit(solution)/shard_map/ppermute | solution.py:10
  71.6 9.1 %psum.15 = bf16[128,128]{1,0:T(8,128)(2,1)} all-reduce(f32[128,128]{1,0:T(8,128)S(1)} %add_bitcast_fusion), channel_id=1, replica_groups=mesh['groups'=2,'ctx'=8,'sub'=2] {'sub'}, use_global_device_ids=true, to_apply=%region_9.10 | all-reduce | flops 16384 | bytes 98304 | tf_op jit(solution)/shard_map/psum | solution.py:147
  80.8 13.4 %all-reduce.2.cloned.1.call-done = f32[128,128]{1,0:T(8,128)} async-done(((f32[128,128]{1,0:T(8,128)}), f32[128,128]{1,0:T(8,128)}) %all-reduce.2.cloned.1.call-update) | async-done | bytes 65552 | tf_op jit(solution)/shard_map/psum | solution.py:147
  94.2 1.5 %multiply_convert_fusion = bf16[128,128]{1,0:T(8,128)(2,1)} fusion(f32[128,128]{1,0:T(8,128)} %all-reduce.2.cloned.1.call-done), kind=kLoop, calls=%fused_computation.51 | loop fusion | flops 32768 | bytes 98304 | tf_op jit(solution)/shard_map/convert_element_type | solution.py:148
  95.8 0.7 copy.43
  (109 shorter events, 13.4 us)
Async XLA Ops:
  7.2 87.0 %all-reduce.2.cloned.1.call-start = ((), (), s32[]{:S(2)}) async-start(), calls=%async_computation | async-start | bytes 131072 | tf_op jit(solution)/shard_map/psum | solution.py:147
  7.2 9.3 %collective-permute-start = (f32[1,4,128]{2,1,0:T(4,128)}, f32[1,4,128]{2,1,0:T(4,128)S(1)}, u32[]{:S(2)}, u32[]{:S(2)}) collective-permute-start(f32[1,4,128]{2,1,0:T(4,128)} %bitcast.110), channel_id=1, source_target_pairs={{0,2},{2,0},{4,6},{6,4},{8,10},{10,8},{12,14},{14,12},{1,3},{3,1},... | collective-permute-start | bytes 6152 | tf_op jit(solution)/shard_map/ppermute | solution.py:10
  9.3 14.9 %collective-permute-start.6 = (bf16[1,128,128]{2,1,0:T(8,128)(2,1)}, bf16[1,128,128]{2,1,0:T(8,128)(2,1)S(1)}, u32[]{:S(2)}, u32[]{:S(2)}) collective-permute-start(bf16[1,128,128]{2,1,0:T(8,128)(2,1)} %bitcast.101), channel_id=1, source_target_pairs={{0,8},{2,10},{4,12},{6,14},{8,0},{10,2},{12,4},{14,6},{1,9},{3,11}... | collective-permute-start | bytes 98312 | tf_op jit(solution)/shard_map/ppermute | solution.py:10
  11.6 1.0 copy-start
  11.6 12.6 %collective-permute-start.9 = (bf16[1,128,128]{2,1,0:T(8,128)(2,1)}, bf16[1,128,128]{2,1,0:T(8,128)(2,1)S(1)}, u32[]{:S(2)}, u32[]{:S(2)}) collective-permute-start(bf16[1,128,128]{2,1,0:T(8,128)(2,1)} %bitcast.103), channel_id=1, source_target_pairs={{0,8},{2,10},{4,12},{6,14},{8,0},{10,2},{12,4},{14,6},{1,9},{3,11}... | collective-permute-start | bytes 98312 | tf_op jit(solution)/shard_map/ppermute | solution.py:10
  13.0 3.4 %copy-start.1 = (bf16[128,512]{1,0:T(8,128)(2,1)S(1)}, bf16[128,512]{1,0:T(8,128)(2,1)}, u32[]{:S(2)}) copy-start(bf16[128,512]{1,0:T(8,128)(2,1)} %param.15) | copy-start | bytes 393220
  13.0 4.1 %collective-permute-start.2 = (f32[1,4,128]{2,1,0:T(4,128)S(1)}, f32[1,4,128]{2,1,0:T(4,128)S(1)}, u32[]{:S(2)}, u32[]{:S(2)}) collective-permute-start(f32[1,4,128]{2,1,0:T(4,128)S(1)} %bitcast.107), channel_id=1, source_target_pairs={{0,2},{2,0},{4,6},{6,4},{8,10},{10,8},{12,14},{14,12},{1,3},{3,1},... | collective-permute-start | bytes 6152 | tf_op jit(solution)/shard_map/ppermute | solution.py:10
  13.4 9.2 %collective-permute-start.7 = (bf16[1,128,512]{1,2,0:T(8,128)(2,1)S(1)}, bf16[1,128,512]{1,2,0:T(8,128)(2,1)S(1)}, u32[]{:S(2)}, u32[]{:S(2)}) collective-permute-start(bf16[1,128,512]{1,2,0:T(8,128)(2,1)S(1)} %bitcast.89), channel_id=1, source_target_pairs={{0,2},{2,0},{4,6},{6,4},{8,10},{10,8},{12,14},{14,12},{1,3},{3,1},... | collective-permute-start | bytes 393224 | tf_op jit(solution)/shard_map/ppermute | solution.py:10
  14.7 0.7 copy-start.5
  16.3 0.7 copy-start.4
  16.5 7.5 %collective-permute-start.4 = (bf16[1,128,512]{1,2,0:T(8,128)(2,1)S(1)}, bf16[1,128,512]{1,2,0:T(8,128)(2,1)S(1)}, u32[]{:S(2)}, u32[]{:S(2)}) collective-permute-start(bf16[1,128,512]{1,2,0:T(8,128)(2,1)S(1)} %bitcast.92), channel_id=1, source_target_pairs={{0,2},{2,0},{4,6},{6,4},{8,10},{10,8},{12,14},{14,12},{1,3},{3,1},... | collective-permute-start | bytes 393224 | tf_op jit(solution)/shard_map/ppermute | solution.py:10
  17.0 2.7 %collective-permute-start.1 = (f32[2,4,128]{2,1,0:T(4,128)S(1)}, f32[2,4,128]{2,1,0:T(4,128)S(1)}, u32[]{:S(2)}, u32[]{:S(2)}) collective-permute-start(f32[2,4,128]{2,1,0:T(4,128)S(1)} %pad_maximum_fusion.8), channel_id=1, source_target_pairs={{0,4},{2,6},{4,0},{6,2},{8,12},{10,14},{12,8},{14,10},{1,5},{3,7},... | collective-permute-start | bytes 12296 | tf_op jit(solution)/shard_map/ppermute | solution.py:10
  19.8 2.8 %collective-permute-start.3 = (f32[2,4,128]{2,1,0:T(4,128)S(1)}, f32[2,4,128]{2,1,0:T(4,128)S(1)}, u32[]{:S(2)}, u32[]{:S(2)}) collective-permute-start(f32[2,4,128]{2,1,0:T(4,128)S(1)} %pad_maximum_fusion.9), channel_id=1, source_target_pairs={{0,4},{2,6},{4,0},{6,2},{8,12},{10,14},{12,8},{14,10},{1,5},{3,7},... | collective-permute-start | bytes 12296 | tf_op jit(solution)/shard_map/ppermute | solution.py:10
  22.6 1.7 %copy-start.2 = (bf16[128,128]{1,0:T(8,128)(2,1)S(1)}, bf16[128,128]{1,0:T(8,128)(2,1)}, u32[]{:S(2)}) copy-start(bf16[128,128]{1,0:T(8,128)(2,1)} %param.16) | copy-start | bytes 98308
  22.6 5.3 %collective-permute-start.8 = (bf16[2,128,512]{1,2,0:T(8,128)(2,1)S(1)}, bf16[2,128,512]{1,2,0:T(8,128)(2,1)S(1)}, u32[]{:S(2)}, u32[]{:S(2)}) collective-permute-start(bf16[2,128,512]{1,2,0:T(8,128)(2,1)S(1)} %pad_maximum_fusion.3), channel_id=1, source_target_pairs={{0,4},{2,6},{4,0},{6,2},{8,12},{10,14},{12,8},{14,10},{1,5},{3,7},... | collective-permute-start | bytes 786440 | tf_op jit(solution)/shard_map/ppermute | solution.py:10
  24.0 0.8 copy-start.3
  24.0 8.3 %collective-permute-start.5 = (bf16[2,128,512]{1,2,0:T(8,128)(2,1)S(1)}, bf16[2,128,512]{1,2,0:T(8,128)(2,1)S(1)}, u32[]{:S(2)}, u32[]{:S(2)}) collective-permute-start(bf16[2,128,512]{1,2,0:T(8,128)(2,1)S(1)} %pad_maximum_fusion.2), channel_id=1, source_target_pairs={{0,4},{2,6},{4,0},{6,2},{8,12},{10,14},{12,8},{14,10},{1,5},{3,7},... | collective-permute-start | bytes 786440 | tf_op jit(solution)/shard_map/ppermute | solution.py:10
  55.6 15.9 %collective-permute-start.10 = (f32[2,128,4,128]{3,1,2,0:T(8,128)S(1)}, f32[2,128,4,128]{3,1,2,0:T(8,128)S(1)}, u32[]{:S(2)}, u32[]{:S(2)}) collective-permute-start(f32[2,128,4,128]{3,1,2,0:T(8,128)S(1)} %slice.67), channel_id=1, source_target_pairs={{0,4},{2,6},{4,0},{6,2},{8,12},{10,14},{12,8},{14,10},{1,5},{3,7},... | collective-permute-start | bytes 1572872 | tf_op jit(solution)/shard_map/ppermute | solution.py:10
  60.9 7.8 %collective-permute-start.12 = (f32[1,128,128]{2,1,0:T(8,128)S(1)}, f32[1,128,128]{2,1,0:T(8,128)S(1)}, u32[]{:S(2)}, u32[]{:S(2)}) collective-permute-start(f32[1,128,128]{2,1,0:T(8,128)S(1)} %slice.71), channel_id=1, source_target_pairs={{0,8},{2,10},{4,12},{6,14},{8,0},{10,2},{12,4},{14,6},{1,9},{3,11}... | collective-permute-start | bytes 196616 | tf_op jit(solution)/shard_map/ppermute | solution.py:10
  63.2 7.0 %collective-permute-start.13 = (f32[1,128,128]{2,1,0:T(8,128)S(1)}, f32[1,128,128]{2,1,0:T(8,128)S(1)}, u32[]{:S(2)}, u32[]{:S(2)}) collective-permute-start(f32[1,128,128]{2,1,0:T(8,128)S(1)} %slice.73), channel_id=1, source_target_pairs={{0,8},{2,10},{4,12},{6,14},{8,0},{10,2},{12,4},{14,6},{1,9},{3,11}... | collective-permute-start | bytes 196616 | tf_op jit(solution)/shard_map/ppermute | solution.py:10
  71.6 24.1 %collective-permute-start.11 = (f32[1,128,4,128]{3,1,2,0:T(8,128)S(1)}, f32[1,128,4,128]{3,1,2,0:T(8,128)S(1)}, u32[]{:S(2)}, u32[]{:S(2)}) collective-permute-start(f32[1,128,4,128]{3,1,2,0:T(8,128)S(1)} %slice.75), channel_id=1, source_target_pairs={{0,2},{2,0},{4,6},{6,4},{8,10},{10,8},{12,14},{14,12},{1,3},{3,1},... | collective-permute-start | bytes 786440 | tf_op jit(solution)/shard_map/ppermute | solution.py:10
Sparse Core Ops, SparseCore 0:
  69.6 24.5 all-reduce.1
where the time goes:
time: 104 us; the launch traced here: 103 us
  waiting for transfers between devices  31 us (30%)
  starting transfers between devices  18.4 us (18%)
  loops' own time  14.5 us (14%)
  between operations  14.2 us (14%)
  local copies, waits for them, and re-layouts  9.37 us (9%)
  blocking collectives  9.15 us (9%)
  other arithmetic  4.08 us (4%)
  matrix products  2.6 us (2%)
    ppermute x14, starting transfers between devices, partner(): return lax.ppermute(value, axis, pairs)  18.4 us
    ppermute x14, waiting for transfers between devices, partner(): return lax.ppermute(value, axis, pairs)  17.6 us
    psum x1, waiting for transfers between devices, per_device(): key_sum, value_sum = lax.psum((key_sum, value_sum), 'sub')  13.4 us
    another operation x1, loops' own time, per_device(): lax.scan(row_sweep, (kv_zero, kv_zero), jnp.arange(row_total, dtype=jnp.i...  13.1 us
    psum x1, blocking collectives, per_device(): key_sum, value_sum = lax.psum((key_sum, value_sum), 'sub')  9.15 us
    unnamed x17, local copies, waits for them, and re-layouts  2.9 us
    dynamic_slice x4, local copies, waits for them, and re-layouts, row_sweep(): row_block = row_blocks[row_index]  2.6 us
    dynamic_slice x4, local copies, waits for them, and re-layouts, per_device(): lax.scan(row_sweep, (kv_zero, kv_zero), jnp.arange(row_total, dtype=jnp.i...  2.35 us
  transfers between devices with their start and end apart: 15, of which 8 were waited for; matrix products, arithmetic and copies ran while one was open for 5% of the time, Pallas kernels for 0%

commit v1 on v0

--- a/solution.py
+++ b/solution.py
@@ -1,6 +1,11 @@
+import functools
+import math
+
 import jax
 import jax.numpy as jnp
 from jax import lax
+from jax.experimental import pallas as pl
+from jax.experimental.pallas import tpu as pltpu
 from jax.sharding import PartitionSpec as P
 
 
@@ -150,6 +155,264 @@
     return (grad_queries, grad_keys, grad_values)
 
 
+MOST_BLOCKS = 16
+MESH = pl.DeviceIdType.MESH
+HIDE = 1e30
+
+
+def fused_kernel(
+    n, heads,
+    q_hbm, k_hbm, v_hbm, o_hbm, g_hbm, l_hbm, place,
+    dq_hbm, dk_hbm, dv_hbm,
+    q_v, o_v, g_v, l_v, kv, qt, gt, qs, gs, ds_all, part, sub_in,
+    x_out, x_in, z_out, z_in, fin, dq_v,
+    load_sem, kz_send, kz_recv, kx_send, kx_recv, ks_send, ks_recv,
+    ps_send, ps_recv, px_send, px_recv, pz_send, pz_recv, fin_sem, out_sem,
+):
+    nz = n // 2
+    tokens, size = k_hbm.shape
+    width = heads * tokens
+    scale = size ** (-0.5)
+    log2e = math.log2(math.e)
+    g = lax.axis_index("groups")
+    t = lax.axis_index("ctx")
+    s = lax.axis_index("sub")
+    z, x = t // 2, t % 2
+    far = [((z + e) % nz) * 2 + x for e in range(nz)]
+    side = [((z + e) % nz) * 2 + (1 - x) for e in range(nz)]
+
+    loads = [
+        pltpu.make_async_copy(k_hbm, kv.at[0, 0], load_sem.at[0]),
+        pltpu.make_async_copy(v_hbm, kv.at[0, 1], load_sem.at[1]),
+        pltpu.make_async_copy(q_hbm, q_v, load_sem.at[2]),
+        pltpu.make_async_copy(g_hbm, g_v, load_sem.at[3]),
+        pltpu.make_async_copy(o_hbm, o_v, load_sem.at[4]),
+        pltpu.make_async_copy(l_hbm, l_v, load_sem.at[5]),
+    ]
+    for load in loads:
+        load.start()
+
+    peers = [(g, far[e], s) for e in range(1, nz)] + [(g, side[0], s), (g, t, 1 - s)]
+    barrier = pltpu.get_barrier_semaphore()
+    for peer in peers:
+        pl.semaphore_signal(barrier, inc=1, device_id=peer, device_id_type=MESH)
+    loads[0].wait()
+    loads[1].wait()
+    pl.semaphore_wait(barrier, len(peers))
+
+    def send(source, target, send_sem, recv_sem, device):
+        copy = pltpu.make_async_remote_copy(
+            src_ref=source, dst_ref=target, send_sem=send_sem, recv_sem=recv_sem,
+            device_id=device, device_id_type=MESH,
+        )
+        copy.start()
+        return copy
+
+    sent = []
+    kz, kx, ks = {}, {}, {}
+    row_order = list(range(1, nz))
+    for e in sorted(row_order, key=lambda e: -min(e, nz - e)):
+        kz[nz - e] = send(
+            kv.at[0, s], kv.at[2 * (nz - e), s], kz_send.at[e], kz_recv.at[nz - e], (g, far[e], s)
+        )
+    kx[0] = send(kv.at[0, s], kv.at[1, s], kx_send.at[0], kx_recv.at[0], (g, side[0], s))
+
+    for load in loads[2:]:
+        load.wait()
+    deltas = []
+    for h in range(heads):
+        here = slice(h * tokens, (h + 1) * tokens)
+        cols = slice(h * size, (h + 1) * size)
+        qs[here, :] = q_v[:, cols]
+        gs[here, :] = g_v[:, cols]
+        qt[:, here] = q_v[:, cols].T
+        grad_t = g_v[:, cols].T
+        gt[:, here] = grad_t
+        out_t = o_v[:, cols].T
+        deltas.append(
+            jnp.sum(grad_t.astype(jnp.float32) * out_t.astype(jnp.float32), axis=0, keepdims=True)
+        )
+    delta_row = jnp.concatenate(deltas, axis=1)
+    lse_row = jnp.concatenate([l_v[h : h + 1, :] for h in range(heads)], axis=1) * log2e
+
+    own_place = place[t]
+    chunk = 2 * tokens if heads % 2 == 0 else tokens
+
+    def score(slot):
+        key_tile, value_tile = kv[slot, 0], kv[slot, 1]
+        lse = lse_row
+        if slot:
+            there = side[slot // 2] if slot % 2 else far[slot // 2]
+            lse = lse + jnp.where(place[there] < own_place, 0.0, HIDE)
+        key_sum = value_sum = None
+        for start in range(0, width, chunk):
+            here = slice(start, start + chunk)
+            scores = jnp.dot(key_tile, qt[:, here], preferred_element_type=jnp.float32)
+            grad_prob = jnp.dot(value_tile, gt[:, here], preferred_element_type=jnp.float32)
+            prob = jnp.exp2(scores * (scale * log2e) - lse[:, here])
+            if slot == 0:
+                shape = (tokens, chunk)
+                key_place = lax.broadcasted_iota(jnp.int32, shape, 0)
+                row_place = lax.broadcasted_iota(jnp.int32, shape, 1) % tokens
+                prob = jnp.where(key_place <= row_place, prob, 0.0)
+            grad_score = (prob * (grad_prob - delta_row[:, here])).astype(jnp.bfloat16)
+            ds_all[slot, :, here] = grad_score
+            value_term = jnp.dot(
+                prob.astype(jnp.bfloat16), gs[here, :], preferred_element_type=jnp.float32
+            )
+            key_term = jnp.dot(grad_score, qs[here, :], preferred_element_type=jnp.float32)
+            value_sum = value_term if value_sum is None else value_sum + value_term
+            key_sum = key_term if key_sum is None else key_sum + key_term
+        part[slot, 0] = key_sum
+        part[slot, 1] = value_sum
+        sent_part[slot] = send(
+            part.at[slot, 1 - s], sub_in.at[slot], ps_send.at[slot], ps_recv.at[slot],
+            (g, t, 1 - s),
+        )
+
+    sent_part = {}
+    px, pz = {}, {}
+
+    def pass_on(slot):
+        sent_part[slot].wait_recv()
+        total = part[slot, s] + sub_in[slot]
+        e = slot // 2
+        if slot % 2:
+            x_out[e] = total.astype(jnp.bfloat16)
+            px[e] = send(x_out.at[e], x_in.at[e], px_send.at[e], px_recv.at[e], (g, side[0], s))
+        else:
+            part[slot, s] = total
+
+    def share(slot):
+        ks[slot] = send(
+            kv.at[slot, s], kv.at[slot, s], ks_send.at[slot], ks_recv.at[slot], (g, t, 1 - s)
+        )
+
+    score(0)
+    near_first = sorted(row_order, key=lambda e: min(e, nz - e))
+    for e in near_first:
+        kz[e].wait_recv()
+        kx[e] = send(
+            kv.at[2 * e, s], kv.at[2 * e + 1, s], kx_send.at[e], kx_recv.at[e], (g, side[0], s)
+        )
+        share(2 * e)
+    kx[0].wait_recv()
+    share(1)
+    order = [1] + [2 * e for e in near_first] + [2 * e + 1 for e in near_first]
+    before = 0
+    waiting = list(near_first)
+    for place_in_order, slot in enumerate(order):
+        ks[slot].wait_recv()
+        score(slot)
+        pass_on(before)
+        before = slot
+        if place_in_order >= 1 and waiting:
+            e = waiting.pop(0)
+            kx[e].wait_recv()
+            share(2 * e + 1)
+    pass_on(before)
+
+    for e in near_first:
+        px[e].wait_recv()
+        z_out[e] = (part[2 * e, s] + x_in[e].astype(jnp.float32)).astype(jnp.bfloat16)
+        pz[nz - e] = send(
+            z_out.at[e], z_in.at[nz - e], pz_send.at[e], pz_recv.at[nz - e], (g, far[e], s)
+        )
+    px[0].wait_recv()
+    total = part[0, s] + x_in[0].astype(jnp.float32)
+
+    keys = kv[:, 0].reshape(n * tokens, size)
+    for start in range(0, width, chunk):
+        grads = ds_all[:, :, start : start + chunk].reshape(n * tokens, chunk)
+        query_t = lax.dot_general(
+            keys, grads, (((0,), (0,)), ((), ())), preferred_element_type=jnp.float32
+        )
+        for first in range(0, chunk, tokens):
+            h = (start + first) // tokens
+            dq_v[:, h * size : (h + 1) * size] = (
+                (query_t[:, first : first + tokens] * scale).T.astype(jnp.bfloat16)
+            )
+    outs = [pltpu.make_async_copy(dq_v, dq_hbm, out_sem.at[0])]
+    outs[0].start()
+
+    for e in near_first:
+        pz[e].wait_recv()
+        total = total + z_in[e].astype(jnp.float32)
+    fin[s] = (total * jnp.where(s == 0, scale, 1.0)).astype(jnp.bfloat16)
+    last = send(fin.at[s], fin.at[s], fin_sem.at[0], fin_sem.at[1], (g, t, 1 - s))
+    last.wait_recv()
+    outs.append(pltpu.make_async_copy(fin.at[0], dk_hbm, out_sem.at[1]))
+    outs.append(pltpu.make_async_copy(fin.at[1], dv_hbm, out_sem.at[2]))
+    outs[1].start()
+    outs[2].start()
+    for group in (kz, kx, ks, sent_part, px, pz):
+        for copy in group.values():
+            copy.wait_send()
+    last.wait_send()
+    for out in outs:
+        out.wait()
+
+
+def fused_device(
+    queries, key_vectors, value_vectors, attn_output, grad_output, row_logsum, block_place
+):
+    n = lax.axis_size("ctx")
+    nz = n // 2
+    tokens, size = key_vectors.shape
+    heads = row_logsum.shape[0]
+    width = heads * tokens
+    half, wide = jnp.bfloat16, jnp.float32
+    dma = pltpu.SemaphoreType.DMA
+    anywhere = pl.BlockSpec(memory_space=pl.ANY)
+    return pl.pallas_call(
+        functools.partial(fused_kernel, n, heads),
+        out_shape=(
+            jax.ShapeDtypeStruct(queries.shape, half),
+            jax.ShapeDtypeStruct(key_vectors.shape, half),
+            jax.ShapeDtypeStruct(value_vectors.shape, half),
+        ),
+        in_specs=[anywhere] * 6 + [pl.BlockSpec(memory_space=pltpu.SMEM)],
+        out_specs=(anywhere,) * 3,
+        scratch_shapes=[
+            pltpu.VMEM(queries.shape, half),
+            pltpu.VMEM(queries.shape, half),
+            pltpu.VMEM(queries.shape, half),
+            pltpu.VMEM(row_logsum.shape, wide),
+            pltpu.VMEM((n, 2, tokens, size), half),
+            pltpu.VMEM((size, width), half),
+            pltpu.VMEM((size, width), half),
+            pltpu.VMEM((width, size), half),
+            pltpu.VMEM((width, size), half),
+            pltpu.VMEM((n, tokens, width), half),
+            pltpu.VMEM((n, 2, tokens, size), wide),
+            pltpu.VMEM((n, tokens, size), wide),
+            pltpu.VMEM((nz, tokens, size), half),
+            pltpu.VMEM((nz, tokens, size), half),
+            pltpu.VMEM((nz, tokens, size), half),
+            pltpu.VMEM((nz, tokens, size), half),
+            pltpu.VMEM((2, tokens, size), half),
+            pltpu.VMEM(queries.shape, half),
+            dma((6,)),
+            dma((nz,)), dma((nz,)),
+            dma((nz,)), dma((nz,)),
+            dma((n,)), dma((n,)),
+            dma((n,)), dma((n,)),
+            dma((nz,)), dma((nz,)),
+            dma((nz,)), dma((nz,)),
+            dma((2,)),
+            dma((3,)),
+        ],
+        compiler_params=pltpu.CompilerParams(
+            collective_id=0, has_side_effects=True, vmem_limit_bytes=32 * 2**20
+        ),
+        cost_estimate=pl.CostEstimate(
+            flops=10 * n * tokens * width * size,
+            bytes_accessed=8 * tokens * width,
+            transcendentals=n * tokens * width,
+        ),
+    )(queries, key_vectors, value_vectors, attn_output, grad_output, row_logsum, block_place)
+
+
 def solution(mesh):
     placed = (
         P(("groups", "ctx"), "sub"),
@@ -160,8 +423,10 @@
         P("sub", ("groups", "ctx")),
         P("groups"),
     )
+    ctx_count = mesh.shape["ctx"]
+    fused = ctx_count % 2 == 0 and 4 <= ctx_count <= MOST_BLOCKS and mesh.shape["sub"] == 2
     return jax.shard_map(
-        per_device,
+        fused_device if fused else per_device,
         mesh=mesh,
         in_specs=placed,
         out_specs=(

time: 104 us -> 33.3 us (0.32)
  waiting for transfers between devices: 31 us -> 0 us
  Pallas kernels: 0 us -> 24.8 us
  starting transfers between devices: 18.4 us -> 0 us
  loops' own time: 14.5 us -> 0 us
  between operations: 14.2 us -> 0.66 us
  blocking collectives: 9.15 us -> 0 us
  other arithmetic: 4.08 us -> 0 us
  matrix products: 2.6 us -> 0 us
  local copies, waits for them, and re-layouts: 9.37 us -> 7.44 us
    pallas_call x0 -> x1, Pallas kernels: none -> 24.8 us  [fused_device(): pl.pallas_call(functools.partial(fused_kernel, n, heads), out_shape=(jax....]
    ppermute x14 -> x0, starting transfers between devices: 18.4 us -> none  [partner(): return lax.ppermute(value, axis, pairs)]
    ppermute x14 -> x0, waiting for transfers between devices: 17.6 us -> none  [partner(): return lax.ppermute(value, axis, pairs)]
    another operation x5 -> x0, loops' own time: 14.5 us -> none  [the longest x1 13.1 us: per_device(): lax.scan(row_sweep, (kv_zero, kv_zero), jnp.arange(row_total, dtype=jnp.i...]
    psum x1 -> x0, waiting for transfers between devices: 13.4 us -> none  [per_device(): key_sum, value_sum = lax.psum((key_sum, value_sum), 'sub')]
    psum x1 -> x0, blocking collectives: 9.15 us -> none  [per_device(): key_sum, value_sum = lax.psum((key_sum, value_sum), 'sub')]
    dynamic_slice x8 -> x0, local copies, waits for them, and re-layouts: 4.95 us -> none  [the longest x4 2.6 us: row_sweep(): row_block = row_blocks[row_index]]
    unnamed x17, local copies, waits for them, and re-layouts: 2.9 us -> 7.44 us
  transfers between devices with their start and end apart: 15 -> 0, of which waited for: 8 -> 0; matrix products, arithmetic and copies ran while one was open for 5% -> 0% of each run, Pallas kernels for 0% -> 0%
where the time goes in v1:
time: 33.3 us; the launch traced here: 32.9 us
  Pallas kernels  24.8 us (74%)
  local copies, waits for them, and re-layouts  7.44 us (22%)
  between operations  0.66 us (2%)
    pallas_call x1, Pallas kernels, fused_device(): pl.pallas_call(functools.partial(fused_kernel, n, heads), out_shape=(jax....  24.8 us
    unnamed x17, local copies, waits for them, and re-layouts  7.44 us

profile of v1, /device:TPU:1, one launch (start us, length us, event | category | flops | bytes accessed | tf_op | source)
XLA Modules:
  0.0 32.9 jit_solution(4235010697251693501)
XLA Ops:
  0.6 0.0 copy-start
  0.6 0.9 %copy-done = bf16[128,512]{1,0:T(8,128)(2,1)S(1)} copy-done((bf16[128,512]{1,0:T(8,128)(2,1)S(1)}, bf16[128,512]{1,0:T(8,128)(2,1)}, u32[]{:S(2)}) %copy-start) | copy-done | bytes 131096
  1.5 0.0 copy-start.1
  1.5 0.9 %copy-done.1 = bf16[128,512]{1,0:T(8,128)(2,1)S(1)} copy-done((bf16[128,512]{1,0:T(8,128)(2,1)S(1)}, bf16[128,512]{1,0:T(8,128)(2,1)}, u32[]{:S(2)}) %copy-start.1) | copy-done | bytes 131096
  2.4 0.0 copy-start.2
  2.4 0.9 %copy-done.2 = bf16[128,512]{1,0:T(8,128)(2,1)S(1)} copy-done((bf16[128,512]{1,0:T(8,128)(2,1)S(1)}, bf16[128,512]{1,0:T(8,128)(2,1)}, u32[]{:S(2)}) %copy-start.2) | copy-done | bytes 131096
  3.3 0.0 copy-start.3
  3.3 0.8 %copy-done.3 = bf16[128,128]{1,0:T(8,128)(2,1)S(1)} copy-done((bf16[128,128]{1,0:T(8,128)(2,1)S(1)}, bf16[128,128]{1,0:T(8,128)(2,1)}, u32[]{:S(2)}) %copy-start.3) | copy-done | bytes 32792
  4.1 0.0 copy-start.4
  4.1 0.8 %copy-done.4 = bf16[128,128]{1,0:T(8,128)(2,1)S(1)} copy-done((bf16[128,128]{1,0:T(8,128)(2,1)S(1)}, bf16[128,128]{1,0:T(8,128)(2,1)}, u32[]{:S(2)}) %copy-start.4) | copy-done | bytes 32792
  4.9 0.0 copy-start.5
  4.9 0.7 %copy-done.5 = f32[4,128]{1,0:T(4,128)S(1)} copy-done((f32[4,128]{1,0:T(4,128)S(1)}, f32[4,128]{1,0:T(4,128)}, u32[]{:S(2)}) %copy-start.5) | copy-done | bytes 2072
  5.5 0.0 copy-start.6
  5.5 0.7 %copy-done.6 = s32[8]{0:T(128)S(1)} copy-done((s32[8]{0:T(128)S(1)}, s32[8]{0:T(128)}, u32[]{:S(2)}) %copy-start.6) | copy-done | bytes 56
  6.2 24.8 %shard_map.94 = (bf16[128,512]{1,0:T(8,128)(2,1)S(1)}, bf16[128,128]{1,0:T(8,128)(2,1)S(1)}, bf16[128,128]{1,0:T(8,128)(2,1)S(1)}) custom-call(bf16[128,512]{1,0:T(8,128)(2,1)S(1)} %copy-done, bf16[128,128]{1,0:T(8,128)(2,1)S(1)} %copy-done.3, bf16[128,128]{1,0:T(8,128)(2,1)S(1)} %copy-done.4, bf16[128,512]{1,0:T(8,128)(2,1)S(1)} %copy-done.1, ...), custom_call_target="tpu_custom_call" | custom-call | flops 671088640 | bytes 524288 | tf_op jit(solution)/shard_map/pallas_call | solution.py:367
  31.1 0.7 %copy.13 = bf16[128,512]{1,0:T(8,128)(2,1)} copy(bf16[128,512]{1,0:T(8,128)(2,1)S(1)} %get-tuple-element.6) | data formatting | bytes 262144
  31.7 0.6 %copy.14 = bf16[128,128]{1,0:T(8,128)(2,1)} copy(bf16[128,128]{1,0:T(8,128)(2,1)S(1)} %get-tuple-element.7) | data formatting | bytes 65536
  32.3 0.6 %copy.15 = bf16[128,128]{1,0:T(8,128)(2,1)} copy(bf16[128,128]{1,0:T(8,128)(2,1)S(1)} %get-tuple-element.8) | data formatting | bytes 65536
Async XLA Ops:
  0.6 0.9 %copy-start = (bf16[128,512]{1,0:T(8,128)(2,1)S(1)}, bf16[128,512]{1,0:T(8,128)(2,1)}, u32[]{:S(2)}) copy-start(bf16[128,512]{1,0:T(8,128)(2,1)} %q_hbm.1) | copy-start | bytes 393220
  1.5 0.9 %copy-start.1 = (bf16[128,512]{1,0:T(8,128)(2,1)S(1)}, bf16[128,512]{1,0:T(8,128)(2,1)}, u32[]{:S(2)}) copy-start(bf16[128,512]{1,0:T(8,128)(2,1)} %o_hbm.1) | copy-start | bytes 393220
  2.4 0.9 %copy-start.2 = (bf16[128,512]{1,0:T(8,128)(2,1)S(1)}, bf16[128,512]{1,0:T(8,128)(2,1)}, u32[]{:S(2)}) copy-start(bf16[128,512]{1,0:T(8,128)(2,1)} %g_hbm.1) | copy-start | bytes 393220
  3.3 0.8 %copy-start.3 = (bf16[128,128]{1,0:T(8,128)(2,1)S(1)}, bf16[128,128]{1,0:T(8,128)(2,1)}, u32[]{:S(2)}) copy-start(bf16[128,128]{1,0:T(8,128)(2,1)} %k_hbm.1) | copy-start | bytes 98308
  4.1 0.8 %copy-start.4 = (bf16[128,128]{1,0:T(8,128)(2,1)S(1)}, bf16[128,128]{1,0:T(8,128)(2,1)}, u32[]{:S(2)}) copy-start(bf16[128,128]{1,0:T(8,128)(2,1)} %v_hbm.1) | copy-start | bytes 98308
  4.9 0.7 %copy-start.5 = (f32[4,128]{1,0:T(4,128)S(1)}, f32[4,128]{1,0:T(4,128)}, u32[]{:S(2)}) copy-start(f32[4,128]{1,0:T(4,128)} %l_hbm.1) | copy-start | bytes 6148
  5.5 0.7 %copy-start.6 = (s32[8]{0:T(128)S(1)}, s32[8]{0:T(128)}, u32[]{:S(2)}) copy-start(s32[8]{0:T(128)} %place.1) | copy-start | bytes 100

commit v2 on v1

--- a/solution.py
+++ b/solution.py
@@ -162,12 +162,12 @@
 
 def fused_kernel(
     n, heads,
-    q_hbm, k_hbm, v_hbm, o_hbm, g_hbm, l_hbm, place,
+    q_hbm, k_hbm, v_hbm, o_hbm, g_hbm, l_hbm, b_hbm,
     dq_hbm, dk_hbm, dv_hbm,
     q_v, o_v, g_v, l_v, kv, qt, gt, qs, gs, ds_all, part, sub_in,
-    x_out, x_in, z_out, z_in, fin, dq_v,
-    load_sem, kz_send, kz_recv, kx_send, kx_recv, ks_send, ks_recv,
-    ps_send, ps_recv, px_send, px_recv, pz_send, pz_recv, fin_sem, out_sem,
+    term_out, term_in, fin, dq_v,
+    place, load_sem, kv_send, kv_recv, ks_send, ks_recv,
+    ps_send, ps_recv, pt_send, pt_recv, fin_sem, out_sem,
 ):
     nz = n // 2
     tokens, size = k_hbm.shape
@@ -178,8 +178,9 @@
     t = lax.axis_index("ctx")
     s = lax.axis_index("sub")
     z, x = t // 2, t % 2
-    far = [((z + e) % nz) * 2 + x for e in range(nz)]
-    side = [((z + e) % nz) * 2 + (1 - x) for e in range(nz)]
+    block = [((z + i // 2) % nz) * 2 + (x + i % 2) % 2 for i in range(n)]
+    mirror = [(nz - i // 2) % nz * 2 + i % 2 for i in range(n)]
+    near_first = sorted(range(1, n), key=lambda i: (min(i // 2, nz - i // 2), i % 2))
 
     loads = [
         pltpu.make_async_copy(k_hbm, kv.at[0, 0], load_sem.at[0]),
@@ -188,11 +189,12 @@
         pltpu.make_async_copy(g_hbm, g_v, load_sem.at[3]),
         pltpu.make_async_copy(o_hbm, o_v, load_sem.at[4]),
         pltpu.make_async_copy(l_hbm, l_v, load_sem.at[5]),
+        pltpu.make_async_copy(b_hbm, place, load_sem.at[6]),
     ]
     for load in loads:
         load.start()
 
-    peers = [(g, far[e], s) for e in range(1, nz)] + [(g, side[0], s), (g, t, 1 - s)]
+    peers = [(g, block[i], s) for i in range(1, n)] + [(g, t, 1 - s)]
     barrier = pltpu.get_barrier_semaphore()
     for peer in peers:
         pl.semaphore_signal(barrier, inc=1, device_id=peer, device_id_type=MESH)
@@ -208,14 +210,11 @@
         copy.start()
         return copy
 
-    sent = []
-    kz, kx, ks = {}, {}, {}
-    row_order = list(range(1, nz))
-    for e in sorted(row_order, key=lambda e: -min(e, nz - e)):
-        kz[nz - e] = send(
-            kv.at[0, s], kv.at[2 * (nz - e), s], kz_send.at[e], kz_recv.at[nz - e], (g, far[e], s)
-        )
-    kx[0] = send(kv.at[0, s], kv.at[1, s], kx_send.at[0], kx_recv.at[0], (g, side[0], s))
+    came, shared, sent_part, passed = {}, {}, {}, {}
+    for i in near_first:
+        came[mirror[i]] = send(
+            kv.at[0, s], kv.at[mirror[i], s], kv_send.at[i], kv_recv.at[mirror[i]], (g, block[i], s)
+        )
 
     for load in loads[2:]:
         load.wait()
@@ -242,8 +241,7 @@
         key_tile, value_tile = kv[slot, 0], kv[slot, 1]
         lse = lse_row
         if slot:
-            there = side[slot // 2] if slot % 2 else far[slot // 2]
-            lse = lse + jnp.where(place[there] < own_place, 0.0, HIDE)
+            lse = lse + jnp.where(place[block[slot]] < own_place, 0.0, HIDE)
         key_sum = value_sum = None
         for start in range(0, width, chunk):
             here = slice(start, start + chunk)
@@ -270,56 +268,36 @@
             (g, t, 1 - s),
         )
 
-    sent_part = {}
-    px, pz = {}, {}
-
     def pass_on(slot):
         sent_part[slot].wait_recv()
         total = part[slot, s] + sub_in[slot]
-        e = slot // 2
-        if slot % 2:
-            x_out[e] = total.astype(jnp.bfloat16)
-            px[e] = send(x_out.at[e], x_in.at[e], px_send.at[e], px_recv.at[e], (g, side[0], s))
-        else:
+        if slot == 0:
             part[slot, s] = total
+            return
+        term_out[slot] = total.astype(jnp.bfloat16)
+        passed[mirror[slot]] = send(
+            term_out.at[slot], term_in.at[mirror[slot]], pt_send.at[slot],
+            pt_recv.at[mirror[slot]], (g, block[slot], s),
+        )
 
     def share(slot):
-        ks[slot] = send(
+        came[slot].wait_recv()
+        shared[slot] = send(
             kv.at[slot, s], kv.at[slot, s], ks_send.at[slot], ks_recv.at[slot], (g, t, 1 - s)
         )
 
     score(0)
-    near_first = sorted(row_order, key=lambda e: min(e, nz - e))
-    for e in near_first:
-        kz[e].wait_recv()
-        kx[e] = send(
-            kv.at[2 * e, s], kv.at[2 * e + 1, s], kx_send.at[e], kx_recv.at[e], (g, side[0], s)
-        )
-        share(2 * e)
-    kx[0].wait_recv()
-    share(1)
-    order = [1] + [2 * e for e in near_first] + [2 * e + 1 for e in near_first]
+    share(near_first[0])
     before = 0
-    waiting = list(near_first)
-    for place_in_order, slot in enumerate(order):
-        ks[slot].wait_recv()
+    for i, slot in enumerate(near_first):
+        if i + 1 < len(near_first):
+            share(near_first[i + 1])
+        shared[slot].wait_recv()
         score(slot)
         pass_on(before)
         before = slot
-        if place_in_order >= 1 and waiting:
-            e = waiting.pop(0)
-            kx[e].wait_recv()
-            share(2 * e + 1)
     pass_on(before)
-
-    for e in near_first:
-        px[e].wait_recv()
-        z_out[e] = (part[2 * e, s] + x_in[e].astype(jnp.float32)).astype(jnp.bfloat16)
-        pz[nz - e] = send(
-            z_out.at[e], z_in.at[nz - e], pz_send.at[e], pz_recv.at[nz - e], (g, far[e], s)
-        )
-    px[0].wait_recv()
-    total = part[0, s] + x_in[0].astype(jnp.float32)
+    total = part[0, s]
 
     keys = kv[:, 0].reshape(n * tokens, size)
     for start in range(0, width, chunk):
@@ -335,9 +313,9 @@
     outs = [pltpu.make_async_copy(dq_v, dq_hbm, out_sem.at[0])]
     outs[0].start()
 
-    for e in near_first:
-        pz[e].wait_recv()
-        total = total + z_in[e].astype(jnp.float32)
+    for slot in near_first:
+        passed[slot].wait_recv()
+        total = total + term_in[slot].astype(jnp.float32)
     fin[s] = (total * jnp.where(s == 0, scale, 1.0)).astype(jnp.bfloat16)
     last = send(fin.at[s], fin.at[s], fin_sem.at[0], fin_sem.at[1], (g, t, 1 - s))
     last.wait_recv()
@@ -345,7 +323,7 @@
     outs.append(pltpu.make_async_copy(fin.at[1], dv_hbm, out_sem.at[2]))
     outs[1].start()
     outs[2].start()
-    for group in (kz, kx, ks, sent_part, px, pz):
+    for group in (came, shared, sent_part, passed):
         for copy in group.values():
             copy.wait_send()
     last.wait_send()
@@ -353,25 +331,30 @@
         out.wait()
 
 
+def settle_kernel(dq_in, dk_in, dv_in, dq_out, dk_out, dv_out):
+    dq_out[...] = dq_in[...]
+    dk_out[...] = dk_in[...]
+    dv_out[...] = dv_in[...]
+
+
 def fused_device(
     queries, key_vectors, value_vectors, attn_output, grad_output, row_logsum, block_place
 ):
     n = lax.axis_size("ctx")
-    nz = n // 2
     tokens, size = key_vectors.shape
     heads = row_logsum.shape[0]
     width = heads * tokens
     half, wide = jnp.bfloat16, jnp.float32
     dma = pltpu.SemaphoreType.DMA
-    anywhere = pl.BlockSpec(memory_space=pl.ANY)
-    return pl.pallas_call(
+    anywhere = pl.BlockSpec(memory_space=pltpu.HBM)
+    grads = pl.pallas_call(
         functools.partial(fused_kernel, n, heads),
         out_shape=(
             jax.ShapeDtypeStruct(queries.shape, half),
             jax.ShapeDtypeStruct(key_vectors.shape, half),
             jax.ShapeDtypeStruct(value_vectors.shape, half),
         ),
-        in_specs=[anywhere] * 6 + [pl.BlockSpec(memory_space=pltpu.SMEM)],
+        in_specs=[anywhere] * 7,
         out_specs=(anywhere,) * 3,
         scratch_shapes=[
             pltpu.VMEM(queries.shape, half),
@@ -386,24 +369,21 @@
             pltpu.VMEM((n, tokens, width), half),
             pltpu.VMEM((n, 2, tokens, size), wide),
             pltpu.VMEM((n, tokens, size), wide),
-            pltpu.VMEM((nz, tokens, size), half),
-            pltpu.VMEM((nz, tokens, size), half),
-            pltpu.VMEM((nz, tokens, size), half),
-            pltpu.VMEM((nz, tokens, size), half),
+            pltpu.VMEM((n, tokens, size), half),
+            pltpu.VMEM((n, tokens, size), half),
             pltpu.VMEM((2, tokens, size), half),
             pltpu.VMEM(queries.shape, half),
-            dma((6,)),
-            dma((nz,)), dma((nz,)),
-            dma((nz,)), dma((nz,)),
+            pltpu.SMEM(block_place.shape, jnp.int32),
+            dma((7,)),
             dma((n,)), dma((n,)),
             dma((n,)), dma((n,)),
-            dma((nz,)), dma((nz,)),
-            dma((nz,)), dma((nz,)),
+            dma((n,)), dma((n,)),
+            dma((n,)), dma((n,)),
             dma((2,)),
             dma((3,)),
         ],
         compiler_params=pltpu.CompilerParams(
-            collective_id=0, has_side_effects=True, vmem_limit_bytes=32 * 2**20
+            collective_id=0, has_side_effects=True, vmem_limit_bytes=60 * 2**20
         ),
         cost_estimate=pl.CostEstimate(
             flops=10 * n * tokens * width * size,
@@ -411,6 +391,10 @@
             transcendentals=n * tokens * width,
         ),
     )(queries, key_vectors, value_vectors, attn_output, grad_output, row_logsum, block_place)
+    return pl.pallas_call(
+        settle_kernel,
+        out_shape=tuple(jax.ShapeDtypeStruct(grad.shape, grad.dtype) for grad in grads),
+    )(*grads)
 
 
 def solution(mesh):

time: 33.3 us -> 25.8 us (0.77)
  local copies, waits for them, and re-layouts: 7.44 us -> 0 us
    unnamed x17 -> x0, local copies, waits for them, and re-layouts: 7.44 us -> none
    pallas_call x0 -> x1, Pallas kernels: none -> 1.6 us  [fused_device(): pl.pallas_call(settle_kernel, out_shape=tuple((jax.ShapeDtypeStruct(grad....]
    pallas_call x1, Pallas kernels: 24.8 us -> 23.4 us  [fused_device(): pl.pallas_call(functools.partial(fused_kernel, n, heads), out_shape=(jax....]
where the time goes in v2:
time: 25.8 us; the launch traced here: 25.6 us
  Pallas kernels  25 us (97%)
  between operations  0.64 us (2%)
    pallas_call x1, Pallas kernels, fused_device(): pl.pallas_call(functools.partial(fused_kernel, n, heads), out_shape=(jax....  23.4 us
    pallas_call x1, Pallas kernels, fused_device(): pl.pallas_call(settle_kernel, out_shape=tuple((jax.ShapeDtypeStruct(grad....  1.6 us

profile of v2, /device:TPU:1, one launch (start us, length us, event | category | flops | bytes accessed | tf_op | source)
XLA Modules:
  0.0 25.6 jit_solution(1212449928682229155)
XLA Ops:
  0.6 23.4 %shard_map.94 = (bf16[128,512]{1,0:T(8,128)(2,1)}, bf16[128,128]{1,0:T(8,128)(2,1)}, bf16[128,128]{1,0:T(8,128)(2,1)}) custom-call(bf16[128,512]{1,0:T(8,128)(2,1)} %q_hbm.1, bf16[128,128]{1,0:T(8,128)(2,1)} %k_hbm.1, bf16[128,128]{1,0:T(8,128)(2,1)} %v_hbm.1, bf16[128,512]{1,0:T(8,128)(2,1)} %o_hbm.1, bf16[128,512]{1,0:T(8,128)(2,1)} %g_hbm.1, ...), custom_call_target="tpu_custom_call" | custom-call | flops 671088640 | bytes 524288 | tf_op jit(solution)/shard_map/pallas_call | solution.py:350
  24.0 1.6 %shard_map.95 = (bf16[128,512]{1,0:T(8,128)(2,1)}, bf16[128,128]{1,0:T(8,128)(2,1)}, bf16[128,128]{1,0:T(8,128)(2,1)}) custom-call(bf16[128,512]{1,0:T(8,128)(2,1)} %get-tuple-element.6.dq_in, bf16[128,128]{1,0:T(8,128)(2,1)} %get-tuple-element.7.dk_in, bf16[128,128]{1,0:T(8,128)(2,1)} %get-tuple-element.8.dv_in), custom_call_target="tpu_custom_call" | custom-call | tf_op jit(solution)/shard_map/pallas_call | solution.py:394

commit v3 on v2

--- a/solution.py
+++ b/solution.py
@@ -180,7 +180,7 @@
     z, x = t // 2, t % 2
     block = [((z + i // 2) % nz) * 2 + (x + i % 2) % 2 for i in range(n)]
     mirror = [(nz - i // 2) % nz * 2 + i % 2 for i in range(n)]
-    near_first = sorted(range(1, n), key=lambda i: (min(i // 2, nz - i // 2), i % 2))
+    near_first = sorted(range(1, n), key=lambda i: (min(i // 2, nz - i // 2), 1 - i % 2))
 
     loads = [
         pltpu.make_async_copy(k_hbm, kv.at[0, 0], load_sem.at[0]),
@@ -191,13 +191,13 @@
         pltpu.make_async_copy(l_hbm, l_v, load_sem.at[5]),
         pltpu.make_async_copy(b_hbm, place, load_sem.at[6]),
     ]
-    for load in loads:
-        load.start()
 
     peers = [(g, block[i], s) for i in range(1, n)] + [(g, t, 1 - s)]
     barrier = pltpu.get_barrier_semaphore()
     for peer in peers:
         pl.semaphore_signal(barrier, inc=1, device_id=peer, device_id_type=MESH)
+    for load in loads:
+        load.start()
     loads[0].wait()
     loads[1].wait()
     pl.semaphore_wait(barrier, len(peers))

time: 25.8 us -> 24.6 us (0.953)
  Pallas kernels: 25 us -> 23.8 us
    pallas_call x1, Pallas kernels: 23.4 us -> 22.2 us  [fused_device(): pl.pallas_call(functools.partial(fused_kernel, n, heads), out_shape=(jax....]
where the time goes in v3:
time: 24.6 us; the launch traced here: 24.4 us
  Pallas kernels  23.8 us (97%)
  between operations  0.64 us (3%)
    pallas_call x1, Pallas kernels, fused_device(): pl.pallas_call(functools.partial(fused_kernel, n, heads), out_shape=(jax....  22.2 us
    pallas_call x1, Pallas kernels, fused_device(): pl.pallas_call(settle_kernel, out_shape=tuple((jax.ShapeDtypeStruct(grad....  1.6 us

profile of v3, /device:TPU:1, one launch (start us, length us, event | category | flops | bytes accessed | tf_op | source)
XLA Modules:
  0.0 24.4 jit_solution(14845846814378820561)
XLA Ops:
  0.6 22.2 %shard_map.94 = (bf16[128,512]{1,0:T(8,128)(2,1)}, bf16[128,128]{1,0:T(8,128)(2,1)}, bf16[128,128]{1,0:T(8,128)(2,1)}) custom-call(bf16[128,512]{1,0:T(8,128)(2,1)} %q_hbm.1, bf16[128,128]{1,0:T(8,128)(2,1)} %k_hbm.1, bf16[128,128]{1,0:T(8,128)(2,1)} %v_hbm.1, bf16[128,512]{1,0:T(8,128)(2,1)} %o_hbm.1, bf16[128,512]{1,0:T(8,128)(2,1)} %g_hbm.1, ...), custom_call_target="tpu_custom_call" | custom-call | flops 671088640 | bytes 524288 | tf_op jit(solution)/shard_map/pallas_call | solution.py:350
  22.8 1.6 %shard_map.95 = (bf16[128,512]{1,0:T(8,128)(2,1)}, bf16[128,128]{1,0:T(8,128)(2,1)}, bf16[128,128]{1,0:T(8,128)(2,1)}) custom-call(bf16[128,512]{1,0:T(8,128)(2,1)} %get-tuple-element.6.dq_in, bf16[128,128]{1,0:T(8,128)(2,1)} %get-tuple-element.7.dk_in, bf16[128,128]{1,0:T(8,128)(2,1)} %get-tuple-element.8.dv_in), custom_call_target="tpu_custom_call" | custom-call | tf_op jit(solution)/shard_map/pallas_call | solution.py:394

commit v4 on v3

--- a/solution.py
+++ b/solution.py
@@ -198,9 +198,6 @@
         pl.semaphore_signal(barrier, inc=1, device_id=peer, device_id_type=MESH)
     for load in loads:
         load.start()
-    loads[0].wait()
-    loads[1].wait()
-    pl.semaphore_wait(barrier, len(peers))
 
     def send(source, target, send_sem, recv_sem, device):
         copy = pltpu.make_async_remote_copy(
@@ -209,12 +206,6 @@
         )
         copy.start()
         return copy
-
-    came, shared, sent_part, passed = {}, {}, {}, {}
-    for i in near_first:
-        came[mirror[i]] = send(
-            kv.at[0, s], kv.at[mirror[i], s], kv_send.at[i], kv_recv.at[mirror[i]], (g, block[i], s)
-        )
 
     for load in loads[2:]:
         load.wait()
@@ -231,6 +222,15 @@
         deltas.append(
             jnp.sum(grad_t.astype(jnp.float32) * out_t.astype(jnp.float32), axis=0, keepdims=True)
         )
+    loads[0].wait()
+    loads[1].wait()
+    pl.semaphore_wait(barrier, len(peers))
+    came, shared, sent_part, passed = {}, {}, {}, {}
+    for i in near_first:
+        came[mirror[i]] = send(
+            kv.at[0, s], kv.at[mirror[i], s], kv_send.at[i], kv_recv.at[mirror[i]], (g, block[i], s)
+        )
+
     delta_row = jnp.concatenate(deltas, axis=1)
     lse_row = jnp.concatenate([l_v[h : h + 1, :] for h in range(heads)], axis=1) * log2e
 

time: 24.6 us -> 25.4 us (1.033)
  Pallas kernels: 23.8 us -> 24.6 us
    pallas_call x1, Pallas kernels: 22.2 us -> 23 us  [fused_device(): pl.pallas_call(functools.partial(fused_kernel, n, heads), out_shape=(jax....]
where the time goes in v4:
time: 25.4 us; the launch traced here: 25.3 us
  Pallas kernels  24.6 us (97%)
  between operations  0.64 us (3%)
    pallas_call x1, Pallas kernels, fused_device(): pl.pallas_call(functools.partial(fused_kernel, n, heads), out_shape=(jax....  23 us
    pallas_call x1, Pallas kernels, fused_device(): pl.pallas_call(settle_kernel, out_shape=tuple((jax.ShapeDtypeStruct(grad....  1.6 us

profile of v4, /device:TPU:1, one launch (start us, length us, event | category | flops | bytes accessed | tf_op | source)
XLA Modules:
  0.0 25.3 jit_solution(16437966620152252342)
XLA Ops:
  0.6 23.0 %shard_map.94 = (bf16[128,512]{1,0:T(8,128)(2,1)}, bf16[128,128]{1,0:T(8,128)(2,1)}, bf16[128,128]{1,0:T(8,128)(2,1)}) custom-call(bf16[128,512]{1,0:T(8,128)(2,1)} %q_hbm.1, bf16[128,128]{1,0:T(8,128)(2,1)} %k_hbm.1, bf16[128,128]{1,0:T(8,128)(2,1)} %v_hbm.1, bf16[128,512]{1,0:T(8,128)(2,1)} %o_hbm.1, bf16[128,512]{1,0:T(8,128)(2,1)} %g_hbm.1, ...), custom_call_target="tpu_custom_call" | custom-call | flops 671088640 | bytes 524288 | tf_op jit(solution)/shard_map/pallas_call | solution.py:350
  23.7 1.6 %shard_map.95 = (bf16[128,512]{1,0:T(8,128)(2,1)}, bf16[128,128]{1,0:T(8,128)(2,1)}, bf16[128,128]{1,0:T(8,128)(2,1)}) custom-call(bf16[128,512]{1,0:T(8,128)(2,1)} %get-tuple-element.6.dq_in, bf16[128,128]{1,0:T(8,128)(2,1)} %get-tuple-element.7.dk_in, bf16[128,128]{1,0:T(8,128)(2,1)} %get-tuple-element.8.dv_in), custom_call_target="tpu_custom_call" | custom-call | tf_op jit(solution)/shard_map/pallas_call | solution.py:394
